TPU v7x, 32 devices: a whole 2x2x4 slice. The times are simulated.
32 devices in a mesh: grid: 16 (over z, y, core), orb: 2 (over x).
Axes of the slice: x: 2, y: 2, z: 4, core: 2. Of those that a mesh axis runs over, the one named last changes fastest.
Arguments:
- orbitals: bfloat16 [4096, 8192], P('grid', 'orb'), may hold values from -6 to 6
- points: int32 [1024], P('grid'), may hold values from 0 to 4095, as said below
Outputs:
- fitted: float32 [4096, 1024], P('grid', 'orb')
- gram: float32 [1024, 1024], P('grid', 'orb')
- density: float32 [1024], P('grid')
Inputs may be any that keep to these rules, and one draw needn't show every extreme that they name: `points`: entries 64 * g to 64 * g + 63 are distinct grid rows of slab g, the rows 256 * g to 256 * g + 255.
All inputs are finite; a program needn't handle non-finite values.
Results may differ from a plain program's by a relative error of at most 0.0003.
Values may be sent and summed in bfloat16 or wider, within the bound.
A program may use at most 64 MiB of HBM per device.

v0:
```python
import jax
import jax.numpy as jnp
from jax import lax
from jax.sharding import PartitionSpec as P

NORB = 8192


def contract(left, right):
    return lax.dot_general(
        left, right, (((1,), (1,)), ((), ())), preferred_element_type=jnp.float32
    )


def on_device(orbitals, points):
    rows = orbitals.shape[0]
    mu_dev = points.shape[0]
    total_mu = mu_dev * lax.axis_size("grid")
    slab_start = lax.axis_index("grid") * rows
    local_rows = points - slab_start
    chosen = jnp.take(orbitals, local_rows, axis=0)
    chosen_wide = chosen.astype(jnp.float32)
    dens_part = jnp.sum(chosen_wide * chosen_wide, axis=1)
    every = lax.all_gather(chosen, "grid", axis=0, tiled=True)
    pair = contract(orbitals, every)
    correlation = contract(chosen, every)
    width = total_mu // lax.axis_size("orb")
    col_start = lax.axis_index("orb") * width
    pair_share, over_share = (
        lax.psum_scatter(pair, "orb", scatter_dimension=1, tiled=True),
        lax.psum_scatter(correlation, "orb", scatter_dimension=1, tiled=True),
    )
    dens_all = lax.psum(dens_part, "orb")
    scale = 1.0 / jnp.sqrt(jnp.float32(NORB))
    fitted = jnp.square(pair_share * scale)
    row_ids = lax.axis_index("grid") * mu_dev + jnp.arange(mu_dev, dtype=jnp.int32)
    col_ids = col_start + jnp.arange(width, dtype=jnp.int32)
    diagonal_mask = row_ids[:, None] == col_ids[None, :]
    gram = jnp.where(diagonal_mask, jnp.float32(0.0), jnp.square(over_share * scale))
    density = dens_all / jnp.float32(NORB)
    return (fitted, gram, density)


def solution(mesh):
    placed = (P("grid", "orb"), P("grid"))
    return jax.shard_map(
        on_device,
        mesh=mesh,
        in_specs=placed,
        out_specs=(P("grid", "orb"), P("grid", "orb"), P("grid")),
        check_vma=False,
    )
```

profile of v0, /device:TPU:0, one launch (start us, length us, event | category | flops | bytes accessed | tf_op | source)
XLA Modules:
  0.0 136.9 jit_solution(10548772775298008019)
XLA Ops:
  7.2 0.0 copy-start
  7.2 0.0 all-gather.2.cloned.1.call-start
  7.2 0.8 compare_and_fusion
  8.0 0.7 copy-done
  8.8 0.9 gather_fusion
  9.6 1.1 multiply_reduce_fusion
  10.8 0.0 all-gather.2.cloned.1.call-update
  10.8 0.0 reduce-scatter.5.cloned.1.call-start
  10.9 77.7 %all-gather.2.cloned.1.call-done = bf16[1024,4096]{1,0:T(8,128)(2,1)} async-done(((bf16[64,4096]{1,0:T(8,128)(2,1)}), bf16[1024,4096]{1,0:T(8,128)(2,1)}) %all-gather.2.cloned.1.call-update) | async-done | bytes 8388624 | tf_op jit(solution)/shard_map/all_gather | solution.py:24
  88.6 6.9 %fusion = f32[64,1024]{1,0:T(8,128)} fusion(bf16[64,4096]{1,0:T(8,128)(2,1)} %get-tuple-element.7, bf16[1024,4096]{1,0:T(8,128)(2,1)} %all-gather.2.cloned.1.call-done), kind=kOutput, calls=%fused_computation.12 | convolution fusion | flops 536870912 | bytes 9175040 | tf_op jit(solution)/shard_map/dot_general | solution.py:10
  95.5 0.0 reduce-scatter.5.cloned.1.call-update
  95.5 0.0 reduce-scatter.3.cloned.1.call-start
  95.6 6.8 %convolution_bitcast_fusion = f32[256,1024]{0,1:T(8,128)} fusion(bf16[1024,4096]{1,0:T(8,128)(2,1)} %all-gather.2.cloned.1.call-done, bf16[256,4096]{1,0:T(8,128)(2,1)S(1)} %copy-done), kind=kOutput, calls=%fused_computation.1 | convolution fusion | flops 2147483648 | bytes 11534336 | tf_op jit(solution)/shard_map/dot_general | solution.py:10
  102.4 0.0 reduce-scatter.3.cloned.1.call-update
  102.4 4.9 %psum.7 = f32[64]{0:T(128)S(1)} all-reduce(f32[64]{0:T(128)S(1)} %get-tuple-element.6), channel_id=1, replica_groups=mesh['grid'=16,'orb'=2] {'orb'}, use_global_device_ids=true, to_apply=%region_3.4 | all-reduce | flops 64 | bytes 512 | tf_op jit(solution)/shard_map/psum | solution.py:33
  107.4 0.5 broadcast_multiply_fusion
  107.9 0.0 reduce-scatter.5.cloned.1.call-done
  107.9 1.6 %multiply_select_fusion = f32[64,512]{1,0:T(8,128)} fusion(f32[64,512]{1,0:T(8,128)} %reduce-scatter.5.cloned.1.call-done, s32[512]{0:T(512)S(1)} %iota_add_fusion, s32[64]{0:T(128)S(1)} %iota_add_fusion.1), kind=kLoop, calls=%fused_computation.5 | loop fusion | flops 131072 | bytes 264448 | tf_op jit(solution)/shard_map/jit(_where)/select_n | solution.py:39
  109.5 18.8 %reduce-scatter.3.cloned.1.call-done = f32[256,512]{0,1:T(8,128)} async-done(((f32[256,1024]{0,1:T(8,128)}), f32[256,512]{0,1:T(8,128)}) %reduce-scatter.3.cloned.1.call-update) | async-done | bytes 524304 | tf_op jit(solution)/shard_map/reduce_scatter | solution.py:30
  128.3 1.1 multiply_multiply_fusion
  129.4 1.0 copy.5
  (3 shorter events, 0.0 us)
Async XLA Ops:
  7.2 1.6 %copy-start = (bf16[256,4096]{1,0:T(8,128)(2,1)S(1)}, bf16[256,4096]{1,0:T(8,128)(2,1)}, u32[]{:S(2)}) copy-start(bf16[256,4096]{1,0:T(8,128)(2,1)} %param.2) | copy-start | bytes 6291460
  7.2 81.4 %all-gather.2.cloned.1.call-start = ((), (), s32[]{:S(2)}) async-start(), calls=%async_computation.2 | async-start | bytes 8912896 | tf_op jit(solution)/shard_map/all_gather | solution.py:24
  10.8 97.1 %reduce-scatter.5.cloned.1.call-start = ((), (), s32[]{:S(2)}) async-start(), calls=%async_computation.4 | async-start | bytes 393216 | tf_op jit(solution)/shard_map/reduce_scatter | solution.py:31
  95.5 32.8 %reduce-scatter.3.cloned.1.call-start = ((), (), s32[]{:S(2)}) async-start(), calls=%async_computation.3 | async-start | bytes 1572864 | tf_op jit(solution)/shard_map/reduce_scatter | solution.py:30
Sparse Core Ops, SparseCore 0:
  10.9 77.5 all-gather.1
  95.6 9.9 reduce-scatter.4
  107.9 20.3 reduce-scatter.2
where the time goes:
time: 137 us
  waiting for transfers between devices  96.6 us (71%)
  matrix products  13.8 us (10%)
  between operations  13.8 us (10%)
  other arithmetic  5.17 us (4%)
  blocking collectives  4.94 us (4%)
  local copies, waits for them, and re-layouts  2.6 us (2%)
    all_gather x1, waiting for transfers between devices, on_device(): every = lax.all_gather(chosen, 'grid', axis=0, tiled=True)  77.7 us
    reduce_scatter x1, waiting for transfers between devices, on_device(): lax.psum_scatter(pair, 'orb', scatter_dimension=1, tiled=True)  18.8 us
    dot_general x2, matrix products, contract(): lax.dot_general(left, right, (((1,), (1,)), ((), ())), preferred_element_...  13.8 us
    psum x1, blocking collectives, on_device(): dens_all = lax.psum(dens_part, 'orb')  4.94 us
  transfers between devices with their start and end apart: 3, of which 2 were waited for; matrix products, arithmetic and copies ran while one was open for 7% of the time, Pallas kernels for 0%

commit v1 on v0

v1 whole, which is shorter than its diff:
```python
import functools
import math

import jax
import jax.numpy as jnp
from jax import lax
from jax.experimental import pallas as pl
from jax.experimental.pallas import tpu as pltpu
from jax.sharding import PartitionSpec as P

MESH = pl.DeviceIdType.MESH
PIECE = 16


def contract(left, right):
    return lax.dot_general(
        left, right, (((1,), (1,)), ((), ())), preferred_element_type=jnp.float32
    )


def kernel(n_grid, n_orb, points_ref, a_ref, fitted_ref, gram_ref, density_ref,
           every, part, got, dens, up_sem, down_sem, side_sem, sib_sem, buddy_sem,
           recv_sem, part_send, part_recv, dens_send, dens_recv):
    rows, depth = a_ref.shape
    mu = every.shape[0] // n_grid
    layers = n_grid // 4
    pieces = mu // PIECE
    half = pieces // 2
    unit = 2 * mu
    local_units = (n_grid * mu) // n_orb // unit
    g = lax.axis_index("grid")
    o = lax.axis_index("orb")
    core, y, z = lax.rem(g, 2), lax.rem(g // 2, 2), g // 4
    buddy = z + 1 - 2 * lax.rem(z, 2)
    first, last = z == 0, z == layers - 1

    def device(zz, yy, cc):
        return zz * 4 + yy * 2 + cc

    barrier = pltpu.get_barrier_semaphore()

    def greet(where):
        pl.semaphore_signal(barrier, inc=1, device_id=where, device_id_type=MESH)

    @pl.when(jnp.logical_not(first))
    def _():
        greet({"grid": device(z - 1, y, core)})

    @pl.when(jnp.logical_not(last))
    def _():
        greet({"grid": device(z + 1, y, core)})

    greet({"grid": device(z, 1 - y, core)})
    greet({"grid": device(z, y, 1 - core)})
    for r in range(1, n_orb):
        greet({"orb": lax.rem(o + r, n_orb)})

    local = points_ref[...] - g * rows
    hot_t = (lax.broadcasted_iota(jnp.int32, (rows, mu), 0) == local).astype(jnp.float32)
    hot = jnp.transpose(hot_t)
    hot_narrow = hot.astype(jnp.bfloat16)
    chunk = min(depth, 1024)
    own_rows = pl.ds(pl.multiple_of(g * mu, mu), mu)

    def pick(k, total):
        cols = pl.ds(pl.multiple_of(k * chunk, chunk), chunk)
        wide = jnp.dot(hot_narrow, a_ref[:, cols], preferred_element_type=jnp.float32)
        every[own_rows, cols] = wide.astype(jnp.bfloat16)
        return total + jnp.sum(wide * wide, axis=1, keepdims=True)

    total = lax.fori_loop(0, depth // chunk, pick, jnp.zeros((mu, 1), jnp.float32))
    dens[o] = jnp.broadcast_to(total, (mu, 128))

    peers = n_orb + 1 + jnp.where(first, 0, 1) + jnp.where(last, 0, 1)
    pl.semaphore_wait(barrier, peers)

    def move(zz, yy, cc, p, target, sem):
        block = device(zz, yy, cc)
        piece = every.at[pl.ds(pl.multiple_of(block * mu + p * PIECE, PIECE), PIECE)]
        return pltpu.make_async_remote_copy(
            src_ref=piece, dst_ref=piece, send_sem=sem, recv_sem=recv_sem.at[block, p],
            device_id={"grid": target}, device_id_type=MESH,
        )

    def begin(copy):
        copy.start()

    def finish(copy):
        copy.wait_send()

    def to_up(zz, p, act):
        @pl.when(jnp.logical_not(last))
        def _():
            act(move(zz, y, core, p, device(z + 1, y, core), up_sem.at[zz, p]))

    def to_down(zz, p, act):
        @pl.when(jnp.logical_not(first))
        def _():
            act(move(zz, y, core, p, device(z - 1, y, core), down_sem.at[zz, p]))

    def to_side(zz, p, act):
        @pl.when(jnp.logical_or(zz != buddy, p >= half))
        def _():
            act(move(zz, y, core, p, device(z, 1 - y, core), side_sem.at[zz, p]))

    def to_sibling(zz, yy, p, act):
        act(move(zz, yy, core, p, device(z, y, 1 - core), sib_sem.at[zz * 2 + yy, p]))

    def to_buddy(p, act):
        act(move(z, 1 - y, core, p, device(buddy, y, core), buddy_sem.at[p]))

    def arrived(zz, yy, cc, p):
        move(zz, yy, cc, p, device(z, y, 1 - core), sib_sem.at[zz * 2 + yy, p]).wait_recv()

    def each(body, count=pieces, start=0):
        lax.fori_loop(start, count, lambda p, _: (body(p), 0)[1], 0)

    def on_layers(s, body):
        if s == 0:
            body(z)
        else:
            @pl.when(z - s >= 0)
            def _():
                body(z - s)

            @pl.when(z + s <= layers - 1)
            def _():
                body(z + s)

    def relay(s, act, wait):
        def below(p):
            if wait:
                arrived(z - s, y, core, p)
            to_up(z - s, p, act)
            to_side(z - s, p, act)
            to_sibling(z - s, y, p, act)

        def above(p):
            if wait:
                arrived(z + s, y, core, p)
            to_down(z + s, p, act)
            to_side(z + s, p, act)
            to_sibling(z + s, y, p, act)

        def both(p):
            @pl.when(z - s >= 0)
            def _():
                below(p)

            @pl.when(z + s <= layers - 1)
            def _():
                above(p)

        each(both)

    def from_side(s, act, wait):
        def one(p):
            def layer(zz):
                @pl.when(jnp.logical_or(zz != buddy, p >= half))
                def _():
                    if wait:
                        arrived(zz, 1 - y, core, p)
                    to_sibling(zz, 1 - y, p, act)

            on_layers(s, layer)

        each(one)

    def part_copy(u):
        owner = u // local_units
        lu = lax.rem(u, local_units)
        slot = lax.rem(o - owner + n_orb, n_orb) - 1
        return pltpu.make_async_remote_copy(
            src_ref=part.at[u], dst_ref=got.at[slot, lu], send_sem=part_send.at[u],
            recv_sem=part_recv.at[slot, lu], device_id={"orb": owner}, device_id_type=MESH,
        )

    def compute(zz, yy):
        each(lambda p: arrived(zz, yy, 1 - core, p))
        u = zz * 2 + yy
        span = pl.ds(pl.multiple_of(u * unit, unit), unit)

        def step(k, acc):
            cols = pl.ds(pl.multiple_of(k * chunk, chunk), chunk)
            return acc + contract(a_ref[:, cols], every[span, cols])

        part[u] = lax.fori_loop(0, depth // chunk, step, jnp.zeros((rows, unit), jnp.float32))

        @pl.when(u // local_units != o)
        def _():
            part_copy(u).start()

    def same_side(s):
        on_layers(s, lambda zz: compute(zz, y))

    def other_side(s, buddies):
        def layer(zz):
            @pl.when((zz == buddy) if buddies else (zz != buddy))
            def _():
                compute(zz, 1 - y)

        on_layers(s, layer)

    def own(act):
        def first_hops(p):
            to_up(z, p, act)
            to_down(z, p, act)
            to_side(z, p, act)

        each(first_hops)
        each(lambda p: to_sibling(z, y, p, act))

    own(begin)

    def dens_copy(r):
        return pltpu.make_async_remote_copy(
            src_ref=dens.at[o], dst_ref=dens.at[o], send_sem=dens_send.at[r - 1],
            recv_sem=dens_recv.at[o], device_id={"orb": lax.rem(o + r, n_orb)},
            device_id_type=MESH,
        )

    for r in range(1, n_orb):
        dens_copy(r).start()

    for s in range(1, layers):
        relay(s, begin, True)
        if s == max(layers - 2, 1):
            from_side(s - 1, begin, True)
            each(lambda p: to_buddy(p, begin), half)
        else:
            from_side(s - 1, begin, True)
        same_side(s - 1)
        if s >= 2:
            other_side(s - 2, False)

    same_side(layers - 1)
    other_side(layers - 2, False)
    from_side(layers - 1, begin, True)

    def buddy_in(act, wait):
        def one(p):
            if wait:
                arrived(buddy, 1 - y, core, p)
            to_sibling(buddy, 1 - y, p, act)

        each(one, half)

    buddy_in(begin, True)
    other_side(layers - 1, False)
    compute(buddy, 1 - y)

    scale = 1.0 / math.sqrt(depth * n_orb)
    for lu in range(local_units):
        u = o * local_units + lu
        pair = part[u]
        for slot in range(n_orb - 1):
            pltpu.make_async_remote_copy(
                src_ref=part.at[u], dst_ref=got.at[slot, lu], send_sem=part_send.at[u],
                recv_sem=part_recv.at[slot, lu], device_id={"orb": lax.rem(o + 1, n_orb)},
                device_id_type=MESH,
            ).wait_recv()
            pair = pair + got[slot, lu]
        cols = slice(lu * unit, (lu + 1) * unit)
        scaled = pair * scale
        fitted_ref[:, cols] = scaled * scaled
        over = jnp.dot(hot, scaled, preferred_element_type=jnp.float32,
                       precision=lax.Precision.HIGHEST)
        row_ids = g * mu + lax.broadcasted_iota(jnp.int32, (mu, unit), 0)
        col_ids = u * unit + lax.broadcasted_iota(jnp.int32, (mu, unit), 1)
        gram_ref[:, cols] = jnp.where(row_ids == col_ids, 0.0, over * over)

    for r in range(1, n_orb):
        peer = lax.rem(o + r, n_orb)
        pltpu.make_async_remote_copy(
            src_ref=dens.at[peer], dst_ref=dens.at[peer], send_sem=dens_send.at[r - 1],
            recv_sem=dens_recv.at[peer], device_id={"orb": peer}, device_id_type=MESH,
        ).wait_recv()
    whole = dens[0]
    for r in range(1, n_orb):
        whole = whole + dens[r]
    density_ref[...] = (jnp.transpose(whole) / jnp.float32(depth * n_orb))[0:1, :]

    own(finish)
    for s in range(1, layers):
        relay(s, finish, False)
        from_side(s - 1, finish, False)
    from_side(layers - 1, finish, False)
    each(lambda p: to_buddy(p, finish), half)
    buddy_in(finish, False)
    for r in range(1, n_orb):
        dens_copy(r).wait_send()

    def left(u, _):
        @pl.when(u // local_units != o)
        def _():
            part_copy(u).wait_send()

        return 0

    lax.fori_loop(0, 2 * layers, left, 0)


def solution(mesh):
    n_grid, n_orb = mesh.shape["grid"], mesh.shape["orb"]

    def on_device(orbitals, points):
        rows, depth = orbitals.shape
        mu = points.shape[0]
        layers = n_grid // 4
        pieces = mu // PIECE
        unit = 2 * mu
        width = n_grid * mu // n_orb
        dma = pltpu.SemaphoreType.DMA
        fitted, gram, density = pl.pallas_call(
            functools.partial(kernel, n_grid, n_orb),
            out_shape=(
                jax.ShapeDtypeStruct((rows, width), jnp.float32),
                jax.ShapeDtypeStruct((mu, width), jnp.float32),
                jax.ShapeDtypeStruct((1, mu), jnp.float32),
            ),
            in_specs=[pl.BlockSpec(memory_space=pltpu.VMEM)] * 2,
            out_specs=(pl.BlockSpec(memory_space=pltpu.VMEM),) * 3,
            scratch_shapes=[
                pltpu.VMEM((n_grid * mu, depth), jnp.bfloat16),
                pltpu.VMEM((2 * layers, rows, unit), jnp.float32),
                pltpu.VMEM((n_orb - 1, width // unit, rows, unit), jnp.float32),
                pltpu.VMEM((n_orb, mu, 128), jnp.float32),
                dma((layers, pieces)),
                dma((layers, pieces)),
                dma((layers, pieces)),
                dma((2 * layers, pieces)),
                dma((pieces,)),
                dma((n_grid, pieces)),
                dma((2 * layers,)),
                dma((n_orb - 1, width // unit)),
                dma((n_orb,)),
                dma((n_orb,)),
            ],
            compiler_params=pltpu.CompilerParams(
                collective_id=0, has_side_effects=True, vmem_limit_bytes=48 * 1024 * 1024
            ),
            cost_estimate=pl.CostEstimate(
                flops=2 * rows * depth * n_grid * mu,
                bytes_accessed=rows * depth * 2 + rows * width * 4,
                transcendentals=0,
            ),
        )(points.reshape(1, mu), orbitals)
        return fitted, gram, density.reshape(mu)

    return jax.shard_map(
        on_device,
        mesh=mesh,
        in_specs=(P("grid", "orb"), P("grid")),
        out_specs=(P("grid", "orb"), P("grid", "orb"), P("grid")),
        check_vma=False,
    )
```

time: 137 us -> 62 us (0.45)
  the two profiles are of different devices: /device:TPU:0 before, /device:TPU:9 now
where the time goes in v1:
time: 62 us; the launch traced here: 61.9 us
  Pallas kernels  57 us (92%)
  local copies, waits for them, and re-layouts  4.2 us (7%)
  between operations  0.65 us (1%)
    pallas_call x1, Pallas kernels, on_device(): pl.pallas_call(functools.partial(kernel, n_grid, n_orb), out_shape=(jax.S...  57 us
    unnamed x7, local copies, waits for them, and re-layouts  4.2 us

profile of v1, /device:TPU:9, one launch (start us, length us, event | category | flops | bytes accessed | tf_op | source)
XLA Modules:
  0.0 61.9 jit_solution(2293261255501496489)
XLA Ops:
  0.6 0.0 copy-start
  0.6 1.6 %copy-done = bf16[256,4096]{1,0:T(8,128)(2,1)S(1)} copy-done((bf16[256,4096]{1,0:T(8,128)(2,1)S(1)}, bf16[256,4096]{1,0:T(8,128)(2,1)}, u32[]{:S(2)}) %copy-start) | copy-done | bytes 2097176
  2.2 0.0 copy-start.1
  2.2 0.7 %copy-done.1 = s32[64]{0:T(128)S(1)} copy-done((s32[64]{0:T(128)S(1)}, s32[64]{0:T(128)}, u32[]{:S(2)}) %copy-start.1) | copy-done | bytes 280
  2.9 57.0 %shard_map.49 = (f32[256,512]{1,0:T(8,128)S(1)}, f32[64,512]{1,0:T(8,128)S(1)}, f32[1,64]{1,0:T(1,128)S(1)}) custom-call(s32[1,64]{1,0:T(1,128)S(1)} %bitcast.2, bf16[256,4096]{1,0:T(8,128)(2,1)S(1)} %copy-done), custom_call_target="tpu_custom_call" | custom-call | flops 2147483648 | bytes 2621440 | tf_op jit(solution)/shard_map/pallas_call | solution.py:314
  59.9 0.8 %copy.8 = f32[256,512]{1,0:T(8,128)} copy(f32[256,512]{1,0:T(8,128)S(1)} %get-tuple-element.12) | data formatting | bytes 1048576
  60.7 0.7 %copy.9 = f32[64,512]{1,0:T(8,128)} copy(f32[64,512]{1,0:T(8,128)S(1)} %get-tuple-element.13) | data formatting | bytes 262144
  61.4 0.5 copy.10
Async XLA Ops:
  0.6 1.6 %copy-start = (bf16[256,4096]{1,0:T(8,128)(2,1)S(1)}, bf16[256,4096]{1,0:T(8,128)(2,1)}, u32[]{:S(2)}) copy-start(bf16[256,4096]{1,0:T(8,128)(2,1)} %a_ref.1) | copy-start | bytes 6291460
  2.2 0.7 %copy-start.1 = (s32[64]{0:T(128)S(1)}, s32[64]{0:T(128)}, u32[]{:S(2)}) copy-start(s32[64]{0:T(128)} %param.3) | copy-start | bytes 772

commit v2 on v1

--- a/solution.py
+++ b/solution.py
@@ -9,7 +9,7 @@
 from jax.sharding import PartitionSpec as P
 
 MESH = pl.DeviceIdType.MESH
-PIECE = 16
+PIECES = 4
 
 
 def contract(left, right):
@@ -18,13 +18,13 @@
     )
 
 
-def kernel(n_grid, n_orb, points_ref, a_ref, fitted_ref, gram_ref, density_ref,
-           every, part, got, dens, up_sem, down_sem, side_sem, sib_sem, buddy_sem,
+def kernel(n_grid, n_orb, points_hbm, a_hbm, pair_ref, hot_ref, density_ref,
+           points_ref, a_ref, load_sem, every, part, got, dens, up_sem, down_sem, side_sem, sib_sem, buddy_sem,
            recv_sem, part_send, part_recv, dens_send, dens_recv):
-    rows, depth = a_ref.shape
-    mu = every.shape[0] // n_grid
+    pieces, rows, chunk = a_ref.shape
+    depth = pieces * chunk
+    mu = every.shape[1] // n_grid
     layers = n_grid // 4
-    pieces = mu // PIECE
     half = pieces // 2
     unit = 2 * mu
     local_units = (n_grid * mu) // n_orb // unit
@@ -37,6 +37,17 @@
     def device(zz, yy, cc):
         return zz * 4 + yy * 2 + cc
 
+    def load(p):
+        return pltpu.make_async_copy(
+            a_hbm.at[:, pl.ds(pl.multiple_of(p * chunk, 128), chunk)], a_ref.at[p],
+            load_sem.at[p],
+        )
+
+    load_points = pltpu.make_async_copy(points_hbm, points_ref, load_sem.at[pieces])
+    load_points.start()
+    for p in range(pieces):
+        load(p).start()
+
     barrier = pltpu.get_barrier_semaphore()
 
     def greet(where):
@@ -55,28 +66,20 @@
     for r in range(1, n_orb):
         greet({"orb": lax.rem(o + r, n_orb)})
 
+    part[...] = jnp.zeros_like(part)
+    load_points.wait()
     local = points_ref[...] - g * rows
     hot_t = (lax.broadcasted_iota(jnp.int32, (rows, mu), 0) == local).astype(jnp.float32)
     hot = jnp.transpose(hot_t)
+    hot_ref[...] = hot
     hot_narrow = hot.astype(jnp.bfloat16)
-    chunk = min(depth, 1024)
     own_rows = pl.ds(pl.multiple_of(g * mu, mu), mu)
 
-    def pick(k, total):
-        cols = pl.ds(pl.multiple_of(k * chunk, chunk), chunk)
-        wide = jnp.dot(hot_narrow, a_ref[:, cols], preferred_element_type=jnp.float32)
-        every[own_rows, cols] = wide.astype(jnp.bfloat16)
-        return total + jnp.sum(wide * wide, axis=1, keepdims=True)
-
-    total = lax.fori_loop(0, depth // chunk, pick, jnp.zeros((mu, 1), jnp.float32))
-    dens[o] = jnp.broadcast_to(total, (mu, 128))
-
     peers = n_orb + 1 + jnp.where(first, 0, 1) + jnp.where(last, 0, 1)
-    pl.semaphore_wait(barrier, peers)
 
     def move(zz, yy, cc, p, target, sem):
         block = device(zz, yy, cc)
-        piece = every.at[pl.ds(pl.multiple_of(block * mu + p * PIECE, PIECE), PIECE)]
+        piece = every.at[p, pl.ds(pl.multiple_of(block * mu, mu), mu)]
         return pltpu.make_async_remote_copy(
             src_ref=piece, dst_ref=piece, send_sem=sem, recv_sem=recv_sem.at[block, p],
             device_id={"grid": target}, device_id_type=MESH,
@@ -153,10 +156,13 @@
 
         each(both)
 
+    def by_side(zz, p):
+        return jnp.logical_or(zz != buddy, p >= half)
+
     def from_side(s, act, wait):
         def one(p):
             def layer(zz):
-                @pl.when(jnp.logical_or(zz != buddy, p >= half))
+                @pl.when(by_side(zz, p))
                 def _():
                     if wait:
                         arrived(zz, 1 - y, core, p)
@@ -164,7 +170,21 @@
 
             on_layers(s, layer)
 
+            if wait:
+                @pl.when(p >= 1)
+                def _():
+                    on_layers(s, lambda zz: side_chunk(zz, p - 1))
+
         each(one)
+        if wait:
+            on_layers(s, lambda zz: side_chunk(zz, pieces - 1))
+
+            def done(zz):
+                @pl.when(zz != buddy)
+                def _():
+                    send_part(zz, 1 - y)
+
+            on_layers(s, done)
 
     def part_copy(u):
         owner = u // local_units
@@ -175,29 +195,28 @@
             recv_sem=part_recv.at[slot, lu], device_id={"orb": owner}, device_id_type=MESH,
         )
 
-    def compute(zz, yy):
-        each(lambda p: arrived(zz, yy, 1 - core, p))
+    def multiply(zz, yy, p):
+        arrived(zz, yy, 1 - core, p)
         u = zz * 2 + yy
         span = pl.ds(pl.multiple_of(u * unit, unit), unit)
-
-        def step(k, acc):
-            cols = pl.ds(pl.multiple_of(k * chunk, chunk), chunk)
-            return acc + contract(a_ref[:, cols], every[span, cols])
-
-        part[u] = lax.fori_loop(0, depth // chunk, step, jnp.zeros((rows, unit), jnp.float32))
+        part[u] += contract(a_ref[p], every[p, span])
+
+    def send_part(zz, yy):
+        u = zz * 2 + yy
 
         @pl.when(u // local_units != o)
         def _():
             part_copy(u).start()
 
+    def side_chunk(zz, p):
+        @pl.when(by_side(zz, p))
+        def _():
+            multiply(zz, 1 - y, p)
+
     def same_side(s):
-        on_layers(s, lambda zz: compute(zz, y))
-
-    def other_side(s, buddies):
         def layer(zz):
-            @pl.when((zz == buddy) if buddies else (zz != buddy))
-            def _():
-                compute(zz, 1 - y)
+            each(lambda p: multiply(zz, y, p))
+            send_part(zz, y)
 
         on_layers(s, layer)
 
@@ -210,7 +229,22 @@
         each(first_hops)
         each(lambda p: to_sibling(z, y, p, act))
 
-    own(begin)
+    def pick(p):
+        load(p).wait()
+        wide = jnp.dot(hot_narrow, a_ref[p], preferred_element_type=jnp.float32)
+        every[p, own_rows] = wide.astype(jnp.bfloat16)
+        return jnp.sum(wide * wide, axis=1, keepdims=True)
+
+    total = pick(0)
+    pl.semaphore_wait(barrier, peers)
+    for p in range(pieces):
+        if p > 0:
+            total = total + pick(p)
+        to_up(z, p, begin)
+        to_down(z, p, begin)
+        to_side(z, p, begin)
+        to_sibling(z, y, p, begin)
+    dens[o] = jnp.broadcast_to(total, (mu, 128))
 
     def dens_copy(r):
         return pltpu.make_async_remote_copy(
@@ -225,29 +259,54 @@
     for s in range(1, layers):
         relay(s, begin, True)
         if s == max(layers - 2, 1):
-            from_side(s - 1, begin, True)
+            if s == 1:
+                from_side(0, begin, True)
             each(lambda p: to_buddy(p, begin), half)
-        else:
-            from_side(s - 1, begin, True)
+            if s == 1:
+                same_side(0)
+                continue
         same_side(s - 1)
-        if s >= 2:
-            other_side(s - 2, False)
+        from_side(s - 1, begin, True)
 
     same_side(layers - 1)
-    other_side(layers - 2, False)
-    from_side(layers - 1, begin, True)
-
-    def buddy_in(act, wait):
-        def one(p):
-            if wait:
-                arrived(buddy, 1 - y, core, p)
-            to_sibling(buddy, 1 - y, p, act)
-
-        each(one, half)
-
-    buddy_in(begin, True)
-    other_side(layers - 1, False)
-    compute(buddy, 1 - y)
+
+    def buddy_in(p, act, wait):
+        if wait:
+            arrived(buddy, 1 - y, core, p)
+        to_sibling(buddy, 1 - y, p, act)
+
+    def tail(p):
+        def layer(zz):
+            @pl.when(by_side(zz, p))
+            def _():
+                arrived(zz, 1 - y, core, p)
+                to_sibling(zz, 1 - y, p, begin)
+
+        on_layers(layers - 1, layer)
+
+        @pl.when(p >= half)
+        def _():
+            buddy_in(p - half, begin, True)
+
+        @pl.when(p >= 1)
+        def _():
+            on_layers(layers - 1, lambda zz: side_chunk(zz, p - 1))
+
+        @pl.when(p >= half + 1)
+        def _():
+            multiply(buddy, 1 - y, p - half - 1)
+
+    each(tail)
+    on_layers(layers - 1, lambda zz: side_chunk(zz, pieces - 1))
+
+    def done(zz):
+        @pl.when(zz != buddy)
+        def _():
+            send_part(zz, 1 - y)
+
+    on_layers(layers - 1, done)
+    multiply(buddy, 1 - y, half - 1)
+    send_part(buddy, 1 - y)
 
     scale = 1.0 / math.sqrt(depth * n_orb)
     for lu in range(local_units):
@@ -261,13 +320,7 @@
             ).wait_recv()
             pair = pair + got[slot, lu]
         cols = slice(lu * unit, (lu + 1) * unit)
-        scaled = pair * scale
-        fitted_ref[:, cols] = scaled * scaled
-        over = jnp.dot(hot, scaled, preferred_element_type=jnp.float32,
-                       precision=lax.Precision.HIGHEST)
-        row_ids = g * mu + lax.broadcasted_iota(jnp.int32, (mu, unit), 0)
-        col_ids = u * unit + lax.broadcasted_iota(jnp.int32, (mu, unit), 1)
-        gram_ref[:, cols] = jnp.where(row_ids == col_ids, 0.0, over * over)
+        pair_ref[:, cols] = pair * scale
 
     for r in range(1, n_orb):
         peer = lax.rem(o + r, n_orb)
@@ -278,7 +331,7 @@
     whole = dens[0]
     for r in range(1, n_orb):
         whole = whole + dens[r]
-    density_ref[...] = (jnp.transpose(whole) / jnp.float32(depth * n_orb))[0:1, :]
+    density_ref[...] = whole / jnp.float32(depth * n_orb)
 
     own(finish)
     for s in range(1, layers):
@@ -286,7 +339,7 @@
         from_side(s - 1, finish, False)
     from_side(layers - 1, finish, False)
     each(lambda p: to_buddy(p, finish), half)
-    buddy_in(finish, False)
+    each(lambda p: buddy_in(p, finish, False), half)
     for r in range(1, n_orb):
         dens_copy(r).wait_send()
 
@@ -298,6 +351,29 @@
         return 0
 
     lax.fori_loop(0, 2 * layers, left, 0)
+
+
+def outputs(pair_hbm, hot_hbm, dens_hbm, fitted_ref, gram_ref, density_ref,
+            pair_ref, hot_ref, dens_ref, sems):
+    loads = [
+        pltpu.make_async_copy(src, dst, sems.at[i])
+        for i, (src, dst) in enumerate(
+            [(pair_hbm, pair_ref), (hot_hbm, hot_ref), (dens_hbm, dens_ref)]
+        )
+    ]
+    for load in loads:
+        load.start()
+    for load in loads:
+        load.wait()
+    mu, width = gram_ref.shape
+    pair = pair_ref[...]
+    fitted_ref[...] = pair * pair
+    over = jnp.dot(hot_ref[...], pair, preferred_element_type=jnp.float32,
+                   precision=lax.Precision.HIGHEST)
+    row_ids = lax.axis_index("grid") * mu + lax.broadcasted_iota(jnp.int32, (mu, width), 0)
+    col_ids = lax.axis_index("orb") * width + lax.broadcasted_iota(jnp.int32, (mu, width), 1)
+    gram_ref[...] = jnp.where(row_ids == col_ids, 0.0, over * over)
+    density_ref[...] = jnp.transpose(dens_ref[...])[0:1, :]
 
 
 def solution(mesh):
@@ -307,21 +383,26 @@
         rows, depth = orbitals.shape
         mu = points.shape[0]
         layers = n_grid // 4
-        pieces = mu // PIECE
+        pieces = PIECES
+        chunk = depth // pieces
         unit = 2 * mu
         width = n_grid * mu // n_orb
         dma = pltpu.SemaphoreType.DMA
-        fitted, gram, density = pl.pallas_call(
+        vmem = pl.BlockSpec(memory_space=pltpu.VMEM)
+        pair, hot, dens = pl.pallas_call(
             functools.partial(kernel, n_grid, n_orb),
             out_shape=(
                 jax.ShapeDtypeStruct((rows, width), jnp.float32),
-                jax.ShapeDtypeStruct((mu, width), jnp.float32),
-                jax.ShapeDtypeStruct((1, mu), jnp.float32),
+                jax.ShapeDtypeStruct((mu, rows), jnp.float32),
+                jax.ShapeDtypeStruct((mu, 128), jnp.float32),
             ),
-            in_specs=[pl.BlockSpec(memory_space=pltpu.VMEM)] * 2,
-            out_specs=(pl.BlockSpec(memory_space=pltpu.VMEM),) * 3,
+            in_specs=[pl.BlockSpec(memory_space=pltpu.HBM)] * 2,
+            out_specs=(vmem,) * 3,
             scratch_shapes=[
-                pltpu.VMEM((n_grid * mu, depth), jnp.bfloat16),
+                pltpu.VMEM((1, mu), jnp.int32),
+                pltpu.VMEM((pieces, rows, chunk), jnp.bfloat16),
+                dma((pieces + 1,)),
+                pltpu.VMEM((pieces, n_grid * mu, chunk), jnp.bfloat16),
                 pltpu.VMEM((2 * layers, rows, unit), jnp.float32),
                 pltpu.VMEM((n_orb - 1, width // unit, rows, unit), jnp.float32),
                 pltpu.VMEM((n_orb, mu, 128), jnp.float32),
@@ -337,7 +418,7 @@
                 dma((n_orb,)),
             ],
             compiler_params=pltpu.CompilerParams(
-                collective_id=0, has_side_effects=True, vmem_limit_bytes=48 * 1024 * 1024
+                collective_id=0, has_side_effects=True, vmem_limit_bytes=60 * 1024 * 1024
             ),
             cost_estimate=pl.CostEstimate(
                 flops=2 * rows * depth * n_grid * mu,
@@ -345,6 +426,23 @@
                 transcendentals=0,
             ),
         )(points.reshape(1, mu), orbitals)
+        fitted, gram, density = pl.pallas_call(
+            outputs,
+            out_shape=(
+                jax.ShapeDtypeStruct((rows, width), jnp.float32),
+                jax.ShapeDtypeStruct((mu, width), jnp.float32),
+                jax.ShapeDtypeStruct((1, mu), jnp.float32),
+            ),
+            in_specs=[pl.BlockSpec(memory_space=pl.ANY)] * 3,
+            out_specs=(vmem,) * 3,
+            scratch_shapes=[
+                pltpu.VMEM((rows, width), jnp.float32),
+                pltpu.VMEM((mu, rows), jnp.float32),
+                pltpu.VMEM((mu, 128), jnp.float32),
+                dma((3,)),
+            ],
+            compiler_params=pltpu.CompilerParams(vmem_limit_bytes=60 * 1024 * 1024),
+        )(pair, hot, dens)
         return fitted, gram, density.reshape(mu)
 
     return jax.shard_map(

time: 62 us -> 60.3 us (0.973)
  the two profiles are of different devices: /device:TPU:9 before, /device:TPU:0 now
where the time goes in v2:
time: 60.3 us; the launch traced here: 60.2 us
  Pallas kernels  59.6 us (99%)
  between operations  0.64 us (1%)
    pallas_call x1, Pallas kernels, on_device(): pl.pallas_call(functools.partial(kernel, n_grid, n_orb), out_shape=(jax.S...  57.3 us
    pallas_call x1, Pallas kernels, on_device(): pl.pallas_call(outputs, out_shape=(jax.ShapeDtypeStruct((rows, width), jn...  2.2 us

profile of v2, /device:TPU:0, one launch (start us, length us, event | category | flops | bytes accessed | tf_op | source)
XLA Modules:
  0.0 60.2 jit_solution(13965394010053699115)
XLA Ops:
  0.6 57.3 %shard_map.49 = (f32[256,512]{1,0:T(8,128)}, f32[64,256]{1,0:T(8,128)}, f32[64,128]{1,0:T(8,128)}) custom-call(s32[1,64]{1,0:T(1,128)} %bitcast.2, bf16[256,4096]{1,0:T(8,128)(2,1)} %a_hbm.1), custom_call_target="tpu_custom_call" | custom-call | flops 2147483648 | bytes 2621440 | tf_op jit(solution)/shard_map/pallas_call | solution.py:392
  58.0 2.2 %shard_map.50 = (f32[256,512]{1,0:T(8,128)}, f32[64,512]{1,0:T(8,128)}, f32[1,64]{1,0:T(1,128)}) custom-call(f32[256,512]{1,0:T(8,128)} %get-tuple-element.9.pair_hbm, f32[64,256]{1,0:T(8,128)} %get-tuple-element.10.hot_hbm, f32[64,128]{1,0:T(8,128)} %get-tuple-element.11.dens_hbm), custom_call_target="tpu_custom_call" | custom-call | tf_op jit(solution)/shard_map/pallas_call | solution.py:429

commit v3 on v2

--- a/solution.py
+++ b/solution.py
@@ -18,7 +18,7 @@
     )
 
 
-def kernel(n_grid, n_orb, points_hbm, a_hbm, pair_ref, hot_ref, density_ref,
+def kernel(n_grid, n_orb, points_hbm, a_hbm, fitted_ref, gram_ref, density_ref,
            points_ref, a_ref, load_sem, every, part, got, dens, up_sem, down_sem, side_sem, sib_sem, buddy_sem,
            recv_sem, part_send, part_recv, dens_send, dens_recv):
     pieces, rows, chunk = a_ref.shape
@@ -71,7 +71,6 @@
     local = points_ref[...] - g * rows
     hot_t = (lax.broadcasted_iota(jnp.int32, (rows, mu), 0) == local).astype(jnp.float32)
     hot = jnp.transpose(hot_t)
-    hot_ref[...] = hot
     hot_narrow = hot.astype(jnp.bfloat16)
     own_rows = pl.ds(pl.multiple_of(g * mu, mu), mu)
 
@@ -308,8 +307,35 @@
     multiply(buddy, 1 - y, half - 1)
     send_part(buddy, 1 - y)
 
+    own(finish)
+    for s in range(1, layers):
+        relay(s, finish, False)
+        from_side(s - 1, finish, False)
+    from_side(layers - 1, finish, False)
+    each(lambda p: to_buddy(p, finish), half)
+    each(lambda p: buddy_in(p, finish, False), half)
+    for r in range(1, n_orb):
+        dens_copy(r).wait_send()
+
+    for r in range(1, n_orb):
+        peer = lax.rem(o + r, n_orb)
+        pltpu.make_async_remote_copy(
+            src_ref=dens.at[peer], dst_ref=dens.at[peer], send_sem=dens_send.at[r - 1],
+            recv_sem=dens_recv.at[peer], device_id={"orb": peer}, device_id_type=MESH,
+        ).wait_recv()
+    whole = dens[0]
+    for r in range(1, n_orb):
+        whole = whole + dens[r]
+    density_ref[...] = (jnp.transpose(whole) / jnp.float32(depth * n_orb))[0:1, :]
+
     scale = 1.0 / math.sqrt(depth * n_orb)
-    for lu in range(local_units):
+    local_layers = local_units // 2
+    row_ids = g * mu + lax.broadcasted_iota(jnp.int32, (mu, unit), 0)
+    lane_ids = lax.broadcasted_iota(jnp.int32, (mu, unit), 1)
+    for j in range(local_units):
+        i = j % local_layers
+        layer = jnp.where(z < layers // 2, i, local_layers - 1 - i)
+        lu = layer * 2 + (y if j < local_layers else 1 - y)
         u = o * local_units + lu
         pair = part[u]
         for slot in range(n_orb - 1):
@@ -319,29 +345,12 @@
                 device_id_type=MESH,
             ).wait_recv()
             pair = pair + got[slot, lu]
-        cols = slice(lu * unit, (lu + 1) * unit)
-        pair_ref[:, cols] = pair * scale
-
-    for r in range(1, n_orb):
-        peer = lax.rem(o + r, n_orb)
-        pltpu.make_async_remote_copy(
-            src_ref=dens.at[peer], dst_ref=dens.at[peer], send_sem=dens_send.at[r - 1],
-            recv_sem=dens_recv.at[peer], device_id={"orb": peer}, device_id_type=MESH,
-        ).wait_recv()
-    whole = dens[0]
-    for r in range(1, n_orb):
-        whole = whole + dens[r]
-    density_ref[...] = whole / jnp.float32(depth * n_orb)
-
-    own(finish)
-    for s in range(1, layers):
-        relay(s, finish, False)
-        from_side(s - 1, finish, False)
-    from_side(layers - 1, finish, False)
-    each(lambda p: to_buddy(p, finish), half)
-    each(lambda p: buddy_in(p, finish, False), half)
-    for r in range(1, n_orb):
-        dens_copy(r).wait_send()
+        cols = pl.ds(pl.multiple_of(lu * unit, unit), unit)
+        scaled = pair * scale
+        fitted_ref[:, cols] = scaled * scaled
+        over = jnp.dot(hot, scaled, preferred_element_type=jnp.float32,
+                       precision=lax.Precision.HIGHEST)
+        gram_ref[:, cols] = jnp.where(row_ids == u * unit + lane_ids, 0.0, over * over)
 
     def left(u, _):
         @pl.when(u // local_units != o)
@@ -353,27 +362,16 @@
     lax.fori_loop(0, 2 * layers, left, 0)
 
 
-def outputs(pair_hbm, hot_hbm, dens_hbm, fitted_ref, gram_ref, density_ref,
-            pair_ref, hot_ref, dens_ref, sems):
-    loads = [
-        pltpu.make_async_copy(src, dst, sems.at[i])
-        for i, (src, dst) in enumerate(
-            [(pair_hbm, pair_ref), (hot_hbm, hot_ref), (dens_hbm, dens_ref)]
-        )
+def copies(a_from, b_from, c_from, a_to, b_to, c_to, sems):
+    moves = [
+        pltpu.make_async_copy(a_from, a_to, sems.at[0]),
+        pltpu.make_async_copy(b_from, b_to, sems.at[1]),
+        pltpu.make_async_copy(c_from, c_to, sems.at[2]),
     ]
-    for load in loads:
-        load.start()
-    for load in loads:
-        load.wait()
-    mu, width = gram_ref.shape
-    pair = pair_ref[...]
-    fitted_ref[...] = pair * pair
-    over = jnp.dot(hot_ref[...], pair, preferred_element_type=jnp.float32,
-                   precision=lax.Precision.HIGHEST)
-    row_ids = lax.axis_index("grid") * mu + lax.broadcasted_iota(jnp.int32, (mu, width), 0)
-    col_ids = lax.axis_index("orb") * width + lax.broadcasted_iota(jnp.int32, (mu, width), 1)
-    gram_ref[...] = jnp.where(row_ids == col_ids, 0.0, over * over)
-    density_ref[...] = jnp.transpose(dens_ref[...])[0:1, :]
+    for move in moves:
+        move.start()
+    for move in moves:
+        move.wait()
 
 
 def solution(mesh):
@@ -389,12 +387,12 @@
         width = n_grid * mu // n_orb
         dma = pltpu.SemaphoreType.DMA
         vmem = pl.BlockSpec(memory_space=pltpu.VMEM)
-        pair, hot, dens = pl.pallas_call(
+        made = pl.pallas_call(
             functools.partial(kernel, n_grid, n_orb),
             out_shape=(
                 jax.ShapeDtypeStruct((rows, width), jnp.float32),
-                jax.ShapeDtypeStruct((mu, rows), jnp.float32),
-                jax.ShapeDtypeStruct((mu, 128), jnp.float32),
+                jax.ShapeDtypeStruct((mu, width), jnp.float32),
+                jax.ShapeDtypeStruct((1, mu), jnp.float32),
             ),
             in_specs=[pl.BlockSpec(memory_space=pltpu.HBM)] * 2,
             out_specs=(vmem,) * 3,
@@ -427,22 +425,13 @@
             ),
         )(points.reshape(1, mu), orbitals)
         fitted, gram, density = pl.pallas_call(
-            outputs,
-            out_shape=(
-                jax.ShapeDtypeStruct((rows, width), jnp.float32),
-                jax.ShapeDtypeStruct((mu, width), jnp.float32),
-                jax.ShapeDtypeStruct((1, mu), jnp.float32),
-            ),
+            copies,
+            out_shape=tuple(jax.ShapeDtypeStruct(m.shape, m.dtype) for m in made),
             in_specs=[pl.BlockSpec(memory_space=pl.ANY)] * 3,
-            out_specs=(vmem,) * 3,
-            scratch_shapes=[
-                pltpu.VMEM((rows, width), jnp.float32),
-                pltpu.VMEM((mu, rows), jnp.float32),
-                pltpu.VMEM((mu, 128), jnp.float32),
-                dma((3,)),
-            ],
+            out_specs=(pl.BlockSpec(memory_space=pl.ANY),) * 3,
+            scratch_shapes=[dma((3,))],
             compiler_params=pltpu.CompilerParams(vmem_limit_bytes=60 * 1024 * 1024),
-        )(pair, hot, dens)
+        )(*made)
         return fitted, gram, density.reshape(mu)
 
     return jax.shard_map(

time: 60.3 us -> 78.6 us (1.30)
  Pallas kernels: 59.6 us -> 77.9 us
    pallas_call x1, Pallas kernels: 2.2 us -> 21 us  [on_device(): pl.pallas_call(copies, out_shape=tuple((jax.ShapeDtypeStruct(m.shape, m.d...]
where the time goes in v3:
time: 78.6 us; the launch traced here: 78.5 us
  Pallas kernels  77.9 us (99%)
    pallas_call x1, Pallas kernels, on_device(): pl.pallas_call(functools.partial(kernel, n_grid, n_orb), out_shape=(jax.S...  56.9 us
    pallas_call x1, Pallas kernels, on_device(): pl.pallas_call(copies, out_shape=tuple((jax.ShapeDtypeStruct(m.shape, m.d...  21 us

profile of v3, /device:TPU:0, one launch (start us, length us, event | category | flops | bytes accessed | tf_op | source)
XLA Modules:
  0.0 78.5 jit_solution(4841553915814324721)
XLA Ops:
  0.6 56.9 %shard_map.49 = (f32[256,512]{1,0:T(8,128)}, f32[64,512]{1,0:T(8,128)}, f32[1,64]{1,0:T(1,128)}) custom-call(s32[1,64]{1,0:T(1,128)} %bitcast.2, bf16[256,4096]{1,0:T(8,128)(2,1)} %a_hbm.1), custom_call_target="tpu_custom_call" | custom-call | flops 2147483648 | bytes 2621440 | tf_op jit(solution)/shard_map/pallas_call | solution.py:390
  57.5 21.0 %shard_map.50 = (f32[256,512]{1,0:T(8,128)}, f32[64,512]{1,0:T(8,128)}, f32[1,64]{1,0:T(1,128)}) custom-call(f32[256,512]{1,0:T(8,128)} %get-tuple-element.9.a_from, f32[64,512]{1,0:T(8,128)} %get-tuple-element.10.b_from, f32[1,64]{1,0:T(1,128)} %get-tuple-element.11.c_from), custom_call_target="tpu_custom_call" | custom-call | tf_op jit(solution)/shard_map/pallas_call | solution.py:427

commit v4 on v3

--- a/solution.py
+++ b/solution.py
@@ -362,16 +362,17 @@
     lax.fori_loop(0, 2 * layers, left, 0)
 
 
-def copies(a_from, b_from, c_from, a_to, b_to, c_to, sems):
-    moves = [
-        pltpu.make_async_copy(a_from, a_to, sems.at[0]),
-        pltpu.make_async_copy(b_from, b_to, sems.at[1]),
-        pltpu.make_async_copy(c_from, c_to, sems.at[2]),
-    ]
-    for move in moves:
-        move.start()
-    for move in moves:
-        move.wait()
+def copies(*refs):
+    sources, targets, held, sems = refs[:3], refs[3:6], refs[6:9], refs[9]
+    loads = [pltpu.make_async_copy(sources[i], held[i], sems.at[i]) for i in range(3)]
+    stores = [pltpu.make_async_copy(held[i], targets[i], sems.at[3 + i]) for i in range(3)]
+    for load in loads:
+        load.start()
+    for load, store in zip(loads, stores):
+        load.wait()
+        store.start()
+    for store in stores:
+        store.wait()
 
 
 def solution(mesh):
@@ -429,7 +430,7 @@
             out_shape=tuple(jax.ShapeDtypeStruct(m.shape, m.dtype) for m in made),
             in_specs=[pl.BlockSpec(memory_space=pl.ANY)] * 3,
             out_specs=(pl.BlockSpec(memory_space=pl.ANY),) * 3,
-            scratch_shapes=[dma((3,))],
+            scratch_shapes=[pltpu.VMEM(m.shape, m.dtype) for m in made] + [dma((6,))],
             compiler_params=pltpu.CompilerParams(vmem_limit_bytes=60 * 1024 * 1024),
         )(*made)
         return fitted, gram, density.reshape(mu)

time: 78.6 us -> 59.6 us (0.76)
  Pallas kernels: 77.9 us -> 58.8 us
    pallas_call x1, Pallas kernels: 21 us -> 1.92 us  [on_device(): pl.pallas_call(copies, out_shape=tuple((jax.ShapeDtypeStruct(m.shape, m.d...]
where the time goes in v4:
time: 59.6 us; the launch traced here: 59.4 us
  Pallas kernels  58.8 us (99%)
  between operations  0.64 us (1%)
    pallas_call x1, Pallas kernels, on_device(): pl.pallas_call(functools.partial(kernel, n_grid, n_orb), out_shape=(jax.S...  56.9 us
    pallas_call x1, Pallas kernels, on_device(): pl.pallas_call(copies, out_shape=tuple((jax.ShapeDtypeStruct(m.shape, m.d...  1.92 us

profile of v4, /device:TPU:0, one launch (start us, length us, event | category | flops | bytes accessed | tf_op | source)
XLA Modules:
  0.0 59.4 jit_solution(11196089789176936560)
XLA Ops:
  0.6 56.9 %shard_map.49 = (f32[256,512]{1,0:T(8,128)}, f32[64,512]{1,0:T(8,128)}, f32[1,64]{1,0:T(1,128)}) custom-call(s32[1,64]{1,0:T(1,128)} %bitcast.2, bf16[256,4096]{1,0:T(8,128)(2,1)} %a_hbm.1), custom_call_target="tpu_custom_call" | custom-call | flops 2147483648 | bytes 2621440 | tf_op jit(solution)/shard_map/pallas_call | solution.py:391
  57.5 1.9 %shard_map.50 = (f32[256,512]{1,0:T(8,128)}, f32[64,512]{1,0:T(8,128)}, f32[1,64]{1,0:T(1,128)}) custom-call(f32[256,512]{1,0:T(8,128)} %get-tuple-element.9.refs_0_, f32[64,512]{1,0:T(8,128)} %get-tuple-element.10.refs_1_, f32[1,64]{1,0:T(1,128)} %get-tuple-element.11.refs_2_), custom_call_target="tpu_custom_call" | custom-call | tf_op jit(solution)/shard_map/pallas_call | solution.py:428
